TPU v7x, 512 devices: a whole 4x8x8 slice. The times are simulated.
512 devices in a mesh: grp: 2 (over core), ep: 128 (over z_lo, x, y), tp: 2 (over z_hi).
Axes of the slice: x: 4, y: 8, z: 8 (z_hi: 2, z_lo: 4; z = z_hi * 4 + z_lo), core: 2. Of those that a mesh axis runs over, the one named last changes fastest.
Arguments:
- master: float32 [2048, 128, 768], P(('grp', 'ep'), None, 'tp'), may hold values from -0.21875 to 0.21875
- gate_up: bfloat16 [128, 2, 2048, 768], P('ep', None, 'grp', 'tp'), may hold values from -0.125 to 0.125
- owner_map: int32 [128], replicated, may hold values from 0 to 127, each once
- tokens: bfloat16 [4, 2048, 2048], P(None, 'ep', 'grp'), may hold values from -6 to 6
- routes: int32 [4, 2048, 8], P(None, 'ep'), may hold values from 0 to 127, all different within a row; in each aligned block of 16 rows (0 to 15, 16 to 31, ..., all dimensions but the last counted through in order) at most 2 rows name the same one
- gate_weights: float32 [4, 2048, 8], P(None, 'ep'), may hold values from 0.1 to 1
Outputs:
- mixed: bfloat16 [4, 2048, 2048], P(None, 'ep', 'grp')
Inputs may be any that keep to these rules, and one draw needn't show every extreme that they name: `owner_map`: each owner index appears exactly once. `routes`: within the rows of one device of one step (aligned blocks of 16 rows) no expert is named by more than 2 rows, a bound that some block reaches in every draw.
All inputs are finite; a program needn't handle non-finite values.
Results may differ from a plain program's by a relative error of at most 0.0049.
Values may be sent and summed in bfloat16 or wider, within the bound.
A program may use at most 64 MiB of HBM per device.

v0:
```python
import functools

import jax
import jax.numpy as jnp
from jax import lax
from jax.experimental import pallas as pl
from jax.experimental.pallas import tpu as pltpu
from jax.sharding import PartitionSpec as P

f32 = jnp.float32
bf16 = jnp.bfloat16
NT = (((1,), (1,)), ((), ()))


def mm(a, b):
    return jnp.dot(a, b, preferred_element_type=f32)


def mm_nt(a, b):
    return lax.dot_general(a, b, NT, preferred_element_type=f32)


def iota(shape, dim):
    return lax.broadcasted_iota(jnp.int32, shape, dim)


def snap(values):
    magnitude = jnp.abs(values)
    spacing = jnp.full_like(magnitude, 2.0 ** (-9))
    inverse = jnp.full_like(magnitude, 2.0**9)
    for exponent in range(-5, 9):
        above = magnitude >= 2.0**exponent
        spacing = jnp.where(above, 2.0 ** (exponent - 3), spacing)
        inverse = jnp.where(above, 2.0 ** (3 - exponent), inverse)
    snapped = jnp.floor(magnitude * inverse + 0.5) * spacing
    return jnp.where(values < 0, -snapped, snapped)


def kernel(
    nz, nx, ny,
    master, gate_up, owner_map, tokens, routes, gates,
    out,
    wt, agw, ag, xs, xr, cmb, part, partr, ys, yr, rs, rr, ts, tr,
    pk, pkr, pk2, pk2r, sa, ra, sb, rb, wd, perm,
    s_ag, s_agw, s_xz, s_grp, s_ret, s_rs, s_tp, s_pk, s_pk2, s_ca, s_cb,
    r_ag, r_agw, r_xz, r_grp, r_ret, r_rs, r_tp, r_pk, r_pk2, r_ca, r_cb,
):
    steps, rows, width = tokens.shape
    experts = owner_map.shape[1]
    top = routes.shape[1]
    depth, _, hid = master.shape
    half_depth = depth // 2
    nq = nz * nx
    slots = 2 * ny
    line = ny * rows
    g = lax.axis_index("grp")
    ep = lax.axis_index("ep")
    t = lax.axis_index("tp")
    z, x, y = ep // (nx * ny), (ep // ny) % nx, ep % ny
    zz = t * nz + z

    def y_peer(dy):
        return {"ep": ep - y + (y + dy + ny) % ny}

    def ring_peer(j, sign):
        dz, dx = j // nx, j % nx
        if 2 * dz < nz:
            off = dz
        elif 2 * dz > nz:
            off = dz - nz
        else:
            off = dz * (1 - 2 * g)
        zt = (zz + sign * off + 2 * nz) % (2 * nz)
        xt = (x + sign * dx + nx) % nx
        return {"ep": (zt % nz) * (nx * ny) + xt * ny + y, "tp": zt // nz}

    def group_peer(j, sign):
        dz, dx = j // nx, j % nx
        zt = (z + sign * dz + nz) % nz
        xt = (x + sign * dx + nx) % nx
        return {"ep": zt * (nx * ny) + xt * ny + y}

    x_mate = {"ep": ep + (1 - 2 * (x % 2)) * ny}
    grp_mate = {"grp": 1 - g}
    tp_mate = {"tp": 1 - t}

    greeted = [y_peer(dy) for dy in range(1, ny)]
    greeted += [ring_peer(j, 1) for j in range(1, nq)]
    greeted += [ring_peer(j, -1) for j in range(1, nq) if 2 * (j // nx) == nz]
    greeted += [group_peer(j, 1) for j in range(nx, nq)]
    greeted += [grp_mate, tp_mate]
    barrier = pltpu.get_barrier_semaphore()
    for peer in greeted:
        pl.semaphore_signal(barrier, inc=1, device_id=peer, device_id_type=pl.DeviceIdType.MESH)

    def send(src, dst, ssem, rsem, peer):
        pltpu.make_async_remote_copy(
            src_ref=src, dst_ref=dst, send_sem=ssem, recv_sem=rsem,
            device_id=peer, device_id_type=pl.DeviceIdType.MESH,
        ).start()

    def await_bytes(ref, sem):
        pltpu.make_async_copy(ref, ref, sem).wait()

    lanes_e = iota((steps * rows, experts), 1)
    weight_of = jnp.zeros((steps * rows, experts), f32)
    for k in range(top):
        weight_of += jnp.where(routes[:, k:k + 1] == lanes_e, gates[:, k:k + 1], 0.0)
    wt[...] = weight_of.reshape(steps, rows, experts)
    pl.semaphore_wait(barrier, len(greeted))

    for dy in range(1, ny):
        send(wt, agw.at[dy], s_agw, r_agw, y_peer(dy))
    agw[0] = weight_of.reshape(steps, rows, experts)

    def gather_start(s, carry):
        for dy in range(1, ny):
            send(tokens.at[s], ag.at[s, dy], s_ag, r_ag.at[s], y_peer(dy))
        ag[s, 0] = tokens[s]
        return carry

    lax.fori_loop(0, steps, gather_start, 0)

    cols = hid // 128
    lanes_p = iota((experts, 128), 1)
    peaks = jnp.zeros((experts, 128), f32)
    for j in range(cols):
        most = jnp.abs(master[0, :, j * 128:(j + 1) * 128])
        for d in range(1, depth):
            most = jnp.maximum(most, jnp.abs(master[d, :, j * 128:(j + 1) * 128]))
        peaks = jnp.where(lanes_p == j, jnp.max(most, axis=1, keepdims=True), peaks)
    pk[...] = peaks.T[:8]
    for dy in range(1, ny):
        send(pk, pkr.at[dy], s_pk, r_pk, y_peer(dy))
    pkr[0] = pk[...]
    await_bytes(pkr.at[pl.ds(1, ny - 1)], r_pk)
    pk2[...] = jnp.max(pkr[...], axis=0)
    send(pk2, pk2r, s_pk2, r_pk2, x_mate)

    row_q = iota((nq * slots, 1), 0)
    peer_q = row_q // slots
    owner_q = (
        ((z + peer_q // nx) % nz) * (nx * ny) + ((x + peer_q % nx) % nx) * ny + y
    )
    pick = (owner_map[...] == owner_q).astype(f32).astype(bf16)
    slot_col = row_q % slots
    slot_row = iota((1, nq * slots), 1) % slots
    row_col = iota((line, 1), 0) // rows
    row_row = iota((1, line), 1) // rows
    la, lb = iota((line, line), 0), iota((line, line), 1)
    lower = ((la // rows == lb // rows) & (lb < la)).astype(f32).astype(bf16)
    spot = ((slot_col // 2) == row_row)
    spot_t = ((slot_row // 2) == row_col)
    order_col = (slot_col % 2 + 1).astype(f32)
    order_row = (slot_row % 2 + 1).astype(f32)

    await_bytes(pk2r, r_pk2)
    both = jnp.maximum(pk2[...], pk2r[...])
    scale_t = (both + 1e-06) / 448.0
    scale = jnp.concatenate([scale_t, jnp.zeros((128 - 8, experts), f32)], axis=0).T

    row_p = iota((experts, 1), 0)
    peer_p = row_p % nq
    owner_p = (
        ((z + peer_p // nx) % nz) * (nx * ny)
        + ((x + peer_p % nx) % nx) * ny
        + (y + row_p // nq) % ny
    )
    order_p = (owner_map[...] == owner_p).astype(f32).astype(bf16)

    def code(d, carry):
        for h in range(2):
            pieces = []
            for j in range(cols):
                own = scale[:, j:j + 1]
                field = master[h * half_depth + d, :, j * 128:(j + 1) * 128]
                pieces.append((snap(field / own) * own).astype(bf16))
            moved = mm(order_p, jnp.concatenate(pieces, axis=1))
            sa[:, h, :, pl.ds(pl.multiple_of(d * hid, 128), hid)] = moved.astype(bf16).reshape(ny, nq, hid)
        return carry

    lax.fori_loop(0, half_depth, code, 0)
    for dy in range(1, ny):
        send(sa.at[dy], ra.at[dy], s_ca, r_ca, y_peer(dy))
    ra[0] = sa[0]
    await_bytes(agw.at[pl.ds(1, ny - 1)], r_agw)

    def dispatch(s):
        weights = agw[:, s].reshape(line, experts)
        named = (weights > 0).astype(f32)
        ahead = mm(lower, named.astype(bf16))
        turn = (named * (ahead + 1.0)).astype(bf16)
        chosen = (mm_nt(pick, turn) == order_col) & spot
        await_bytes(ag.at[s, pl.ds(1, ny - 1)], r_ag.at[s])
        moved = mm(chosen.astype(f32).astype(bf16), ag[s].reshape(line, width))
        moved = moved.astype(bf16).reshape(nq, slots, width)
        xs[s] = moved
        for j in range(1, nq):
            send(xs.at[s, j], xr.at[s, j], s_xz, r_xz.at[s], ring_peer(j, 1))
        xr[s, 0] = xs[s, 0]
        kept = (mm_nt(turn, pick) == order_row) & spot_t
        upper = weights.astype(bf16)
        rest = (weights - upper.astype(f32)).astype(bf16)
        cmb[s, 0] = jnp.where(kept, mm_nt(upper, pick), 0.0).astype(bf16)
        cmb[s, 1] = jnp.where(kept, mm_nt(rest, pick), 0.0).astype(bf16)

    def regroup():
        a, b = iota((2 * experts, 2 * experts), 0), iota((2 * experts, 2 * experts), 1)
        j, dy, h = a // (2 * ny), (a // 2) % ny, a % 2
        order = (b == (dy * 2 + h) * nq + j).astype(f32).astype(bf16)
        await_bytes(ra.at[pl.ds(1, ny - 1)], r_ca)
        moved = mm(order, ra[...].reshape(2 * experts, half_depth * hid))
        sb[...] = moved.astype(bf16).reshape(nq, 2 * ny, half_depth * hid)
        for j in range(1, nq):
            send(sb.at[j], rb.at[j], s_cb, r_cb, group_peer(j, 1))
        rb[0] = sb[0]
        c = iota((1, 2 * experts), 1)
        j, dy, h = c // (2 * ny), (c // 2) % ny, c % 2
        source = (
            ((z - j // nx + nz) % nz) * (nx * ny) + ((x - j % nx + nx) % nx) * ny + (y - dy + ny) % ny
        )
        base = source * depth + h * half_depth
        feature = iota((width, 1), 0)
        for d in range(half_depth):
            perm[:, d * 2 * experts:(d + 1) * 2 * experts] = (feature == base + d).astype(f32).astype(bf16)

    def place():
        await_bytes(rb.at[pl.ds(1, nq - 1)], r_cb)
        total = jnp.zeros((width, hid), f32)
        for d in range(half_depth):
            total += mm(
                perm[:, d * 2 * experts:(d + 1) * 2 * experts],
                rb[:, :, d * hid:(d + 1) * hid].reshape(2 * experts, hid),
            )
        wd[...] = total.astype(bf16)

    def expert_in(s):
        await_bytes(xr.at[s, pl.ds(1, nq - 1)], r_xz.at[s])
        items = xr[s].reshape(nq * slots, width)
        part[s, 0] = mm(items, gate_up[0])
        part[s, 1] = mm(items, gate_up[1])
        send(part.at[s], partr.at[s], s_grp, r_grp.at[s], grp_mate)

    def expert_out(s):
        await_bytes(partr.at[s], r_grp.at[s])
        gated = part[s, 0] + partr[s, 0]
        upped = part[s, 1] + partr[s, 1]
        hidden = (gated / (1.0 + jnp.exp(-gated)) * upped).astype(bf16)
        result = mm_nt(hidden, wd[...])
        ys[s] = result.astype(bf16).reshape(nq, slots, width)
        for j in range(1, nq):
            send(ys.at[s, j], yr.at[s, j], s_ret, r_ret.at[s], ring_peer(j, -1))
        yr[s, 0] = ys[s, 0]

    def combine(s):
        await_bytes(yr.at[s, pl.ds(1, nq - 1)], r_ret.at[s])
        items = yr[s].reshape(nq * slots, width)
        mixed = mm(cmb[s, 0], items) + mm(cmb[s, 1], items)
        rs[s] = mixed.astype(bf16).reshape(ny, rows, width)
        for dy in range(1, ny):
            send(rs.at[s, dy], rr.at[s, dy], s_rs, r_rs.at[s], y_peer(-dy))
        rr[s, 0] = rs[s, 0]

    def total(s):
        await_bytes(rr.at[s, pl.ds(1, ny - 1)], r_rs.at[s])
        mixed = rr[s, 0].astype(f32)
        for dy in range(1, ny):
            mixed += rr[s, dy].astype(f32)
        ts[s] = mixed.astype(bf16)
        send(ts.at[s], tr.at[s], s_tp, r_tp.at[s], tp_mate)

    def turn_of(i, carry):
        @pl.when(i < steps)
        def _():
            dispatch(i)

        @pl.when(i == 0)
        def _():
            regroup()

        @pl.when((i >= 1) & (i <= steps))
        def _():
            expert_in(i - 1)

        @pl.when(i == 1)
        def _():
            place()

        @pl.when((i >= 1) & (i <= steps))
        def _():
            expert_out(i - 1)

        @pl.when((i >= 2) & (i <= steps + 1))
        def _():
            combine(i - 2)

        @pl.when(i >= 3)
        def _():
            total(i - 3)

        return carry

    lax.fori_loop(0, steps + 3, turn_of, 0)

    def finish(s, carry):
        await_bytes(tr.at[s], r_tp.at[s])
        out[s] = (ts[s].astype(f32) + tr[s].astype(f32)).astype(bf16)
        return carry

    lax.fori_loop(0, steps, finish, 0)

    rest_y, rest_q = pl.ds(1, ny - 1), pl.ds(1, nq - 1)
    await_bytes(agw.at[rest_y], s_agw)
    await_bytes(ag.at[:, rest_y], s_ag)
    await_bytes(pkr.at[rest_y], s_pk)
    await_bytes(pk2r, s_pk2)
    await_bytes(ra.at[rest_y], s_ca)
    await_bytes(rb.at[rest_q], s_cb)
    await_bytes(xr.at[:, rest_q], s_xz)
    await_bytes(partr, s_grp)
    await_bytes(yr.at[:, rest_q], s_ret)
    await_bytes(rr.at[:, rest_y], s_rs)
    await_bytes(tr, s_tp)


def on_device(nz, nx, ny, master, gate_up, owner_map, tokens, routes, gate_weights):
    steps, rows, width = tokens.shape
    depth, experts, hid = master.shape
    top = routes.shape[2]
    nq = nz * nx
    slots = 2 * ny
    line = ny * rows
    vmem = pltpu.VMEM
    dma = pltpu.SemaphoreType.DMA
    scratch = [
        vmem((steps, rows, experts), f32),
        vmem((ny, steps, rows, experts), f32),
        vmem((steps, ny, rows, width), bf16),
        vmem((steps, nq, slots, width), bf16),
        vmem((steps, nq, slots, width), bf16),
        vmem((steps, 2, line, nq * slots), bf16),
        vmem((steps, 2, nq * slots, hid), f32),
        vmem((steps, 2, nq * slots, hid), f32),
        vmem((steps, nq, slots, width), bf16),
        vmem((steps, nq, slots, width), bf16),
        vmem((steps, ny, rows, width), bf16),
        vmem((steps, ny, rows, width), bf16),
        vmem((steps, rows, width), bf16),
        vmem((steps, rows, width), bf16),
        vmem((8, experts), f32),
        vmem((ny, 8, experts), f32),
        vmem((8, experts), f32),
        vmem((8, experts), f32),
        vmem((ny, 2, nq, depth // 2 * hid), bf16),
        vmem((ny, 2, nq, depth // 2 * hid), bf16),
        vmem((nq, 2 * ny, depth // 2 * hid), bf16),
        vmem((nq, 2 * ny, depth // 2 * hid), bf16),
        vmem((width, hid), bf16),
        vmem((width, width), bf16),
    ]
    scratch += [dma] * 11
    scratch += [
        dma((steps,)), dma, dma((steps,)), dma((steps,)), dma((steps,)), dma((steps,)), dma((steps,)),
        dma, dma, dma, dma,
    ]
    return pl.pallas_call(
        functools.partial(kernel, nz, nx, ny),
        out_shape=jax.ShapeDtypeStruct((steps, rows, width), bf16),
        in_specs=[pl.BlockSpec(memory_space=vmem)] * 6,
        out_specs=pl.BlockSpec(memory_space=vmem),
        scratch_shapes=scratch,
        compiler_params=pltpu.CompilerParams(
            collective_id=0, has_side_effects=True, vmem_limit_bytes=56 * 2**20
        ),
    )(
        master,
        gate_up[0],
        owner_map.reshape(1, experts),
        tokens,
        routes.reshape(steps * rows, top),
        gate_weights.reshape(steps * rows, top),
    )


def solution(mesh, sizes=(4, 4, 8)):
    placed = (
        P(("grp", "ep"), None, "tp"),
        P("ep", None, "grp", "tp"),
        P(),
        P(None, "ep", "grp"),
        P(None, "ep", None),
        P(None, "ep", None),
    )
    return jax.shard_map(
        functools.partial(on_device, *sizes),
        mesh=mesh, in_specs=placed, out_specs=P(None, "ep", "grp"), check_vma=False,
    )
```

profile of v0, /device:TPU:1, one launch (start us, length us, event | category | flops | bytes accessed | tf_op | source)
XLA Modules:
  0.0 153.3 jit_solution(12533608682974022911)
XLA Ops:
  0.0 1.4 copy.7
  1.4 1.4 copy.8
  2.8 148.9 %shard_map.64 = bf16[4,16,1024]{2,1,0:T(8,128)(2,1)} custom-call(f32[8,128,384]{2,1,0:T(8,128)} %master.1, bf16[2,1024,384]{2,1,0:T(8,128)(2,1)} %bitcast.4, s32[1,128]{1,0:T(1,128)} %bitcast.7, bf16[4,16,1024]{2,1,0:T(8,128)(2,1)} %tokens.1, s32[64,8]{1,0:T(8,128)} %bitcast.5, f32[64,8]{1,0:T(8,128)} %bitcast.6), custom_call_target="tpu_custom_call" | custom-call | tf_op jit(solution)/shard_map/pallas_call | solution.py:366
  151.7 1.6 %copy.10 = bf16[4,16,1024]{2,1,0:T(8,128)(2,1)} copy(bf16[4,16,1024]{2,1,0:T(8,128)(2,1)} %shard_map.64) | data formatting | bytes 262144
where the time goes:
time: 154 us; the launch traced here: 153 us
  Pallas kernels  149 us (97%)
  local copies, waits for them, and re-layouts  4.36 us (3%)
    pallas_call x1, Pallas kernels, on_device(): pl.pallas_call(functools.partial(kernel, nz, nx, ny), out_shape=jax.Shape...  149 us
    unnamed x3, local copies, waits for them, and re-layouts  4.36 us

commit v1 on v0

v1 whole, which is shorter than its diff:
```python
import functools

import jax
import jax.numpy as jnp
from jax import lax
from jax.experimental import pallas as pl
from jax.experimental.pallas import tpu as pltpu
from jax.sharding import PartitionSpec as P

f32 = jnp.float32
bf16 = jnp.bfloat16
NT = (((1,), (1,)), ((), ()))


def mm(a, b):
    return jnp.dot(a, b, preferred_element_type=f32)


def mm_nt(a, b):
    return lax.dot_general(a, b, NT, preferred_element_type=f32)


def iota(shape, dim):
    return lax.broadcasted_iota(jnp.int32, shape, dim)


def snap(values):
    magnitude = jnp.abs(values)
    magnitude = magnitude + magnitude * 2.0 ** (-22)
    large = magnitude * (2.0**20 + 1.0)
    fine = large - (large - magnitude)
    coarse = (magnitude + 24576.0) - 24576.0
    snapped = jnp.where(magnitude < 2.0 ** (-5), coarse, fine)
    return jnp.where(values < 0, -snapped, snapped)


def kernel(
    nz, nx, ny,
    master, gate_up, owner_map, tokens, routes, gates,
    out,
    wt, agw, ag, xs, x1, xr, cmb, part, partr, hd, ys, z1, yr, rs, rr, ts, tr,
    pk, pkr, pk2, pk2r, sa, c1, c2, sb, rb, wd,
    s_ag, s_agw, s_x, s_z, s_grp, s_rz, s_rx, s_rs, s_tp, s_pk, s_pk2, s_cx, s_cz, s_cy,
    r_ag, r_agw, r_x, r_z, r_grp, r_rz, r_rx, r_rs, r_tp, r_pk, r_pk2, r_cx, r_cz, r_cy,
):
    steps, rows, width = tokens.shape
    experts = owner_map.shape[1]
    top = routes.shape[1]
    depth, _, hid = master.shape
    parts = depth // 2
    nq = nz * nx
    slots = 2 * ny
    line = ny * rows
    g = lax.axis_index("grp")
    ep = lax.axis_index("ep")
    t = lax.axis_index("tp")
    z, x, y = ep // (nx * ny), (ep // ny) % nx, ep % ny
    zz = t * nz + z

    def y_peer(dy):
        return {"ep": ep - y + (y + dy + ny) % ny}

    def x_peer(dx):
        return {"ep": ep + ((x + dx + nx) % nx - x) * ny}

    def ring_peer(dz, sign):
        if 2 * dz < nz:
            off = dz
        elif 2 * dz > nz:
            off = dz - nz
        else:
            off = dz * (1 - 2 * g)
        zt = (zz + sign * off + 2 * nz) % (2 * nz)
        return {"ep": ep + (zt % nz - z) * (nx * ny), "tp": zt // nz}

    def group_peer(dz):
        return {"ep": ep + ((z + dz) % nz - z) * (nx * ny)}

    x_mate = {"ep": ep + (1 - 2 * (x % 2)) * ny}
    grp_mate = {"grp": 1 - g}
    tp_mate = {"tp": 1 - t}

    greeted = [y_peer(dy) for dy in range(1, ny)]
    greeted += [x_peer(dx) for dx in range(1, nx)]
    greeted += [ring_peer(dz, 1) for dz in range(1, nz)]
    greeted += [ring_peer(nz // 2, -1)]
    greeted += [group_peer(dz) for dz in range(1, nz)]
    greeted += [grp_mate, tp_mate]
    barrier = pltpu.get_barrier_semaphore()
    for peer in greeted:
        pl.semaphore_signal(barrier, inc=1, device_id=peer, device_id_type=pl.DeviceIdType.MESH)

    def send(src, dst, ssem, rsem, peer):
        pltpu.make_async_remote_copy(
            src_ref=src, dst_ref=dst, send_sem=ssem, recv_sem=rsem,
            device_id=peer, device_id_type=pl.DeviceIdType.MESH,
        ).start()

    def await_bytes(ref, sem):
        pltpu.make_async_copy(ref, ref, sem).wait()

    rest_x, rest_y, rest_z = pl.ds(1, nx - 1), pl.ds(1, ny - 1), pl.ds(1, nz - 1)

    cols = hid // 128
    lanes_p = iota((experts, 128), 1)
    peaks = jnp.zeros((experts, 128), f32)
    for j in range(cols):
        most = jnp.abs(master[0, :, j * 128:(j + 1) * 128])
        for d in range(1, depth):
            most = jnp.maximum(most, jnp.abs(master[d, :, j * 128:(j + 1) * 128]))
        peaks = jnp.where(lanes_p == j, jnp.max(most, axis=1, keepdims=True), peaks)
    pk[...] = peaks.T[:8]
    pkr[0] = pk[...]

    count = steps * rows
    blank = [jnp.zeros((top, experts - count), f32)]
    names = jnp.concatenate([routes[s].astype(f32) for s in range(steps)] + blank, axis=1)
    shares = jnp.concatenate([gates[s] for s in range(steps)] + blank, axis=1)
    index_e = iota((experts, experts), 0).astype(f32)
    weight_of = jnp.zeros((experts, experts), f32)
    for k in range(top):
        weight_of += jnp.where(names[k:k + 1, :] == index_e, shares[k:k + 1, :], 0.0)
    weight_of = weight_of.T[:count].reshape(steps, rows, experts)
    wt[...] = weight_of
    agw[0] = weight_of
    pl.semaphore_wait(barrier, len(greeted))

    for dy in range(1, ny):
        send(pk, pkr.at[dy], s_pk, r_pk, y_peer(dy))

    def gather_start(s, carry):
        for dy in range(1, ny):
            send(tokens.at[s], ag.at[s, dy], s_ag, r_ag.at[s], y_peer(dy))
        ag[s, 0] = tokens[s]
        return carry

    gather_start(0, 0)
    for dy in range(1, ny):
        send(wt, agw.at[dy], s_agw, r_agw, y_peer(dy))

    await_bytes(pkr.at[rest_y], r_pk)
    pk2[...] = jnp.max(pkr[...], axis=0)
    send(pk2, pk2r, s_pk2, r_pk2, x_mate)
    lax.fori_loop(1, steps, gather_start, 0)

    row_q = iota((nq * slots, 1), 0)
    peer_q = row_q // slots
    owner_q = (
        ((z + peer_q % nz) % nz) * (nx * ny) + ((x + peer_q // nz) % nx) * ny + y
    )
    pick = (owner_map[...] == owner_q).astype(f32).astype(bf16)
    slot_col = row_q % slots
    slot_row = iota((1, nq * slots), 1) % slots
    row_col = iota((line, 1), 0) // rows
    row_row = iota((1, line), 1) // rows
    la, lb = iota((line, line), 0), iota((line, line), 1)
    lower = ((la // rows == lb // rows) & (lb < la)).astype(f32).astype(bf16)
    spot = ((slot_col // 2) == row_row)
    spot_t = ((slot_row // 2) == row_col)
    order_col = (slot_col % 2 + 1).astype(f32)
    order_row = (slot_row % 2 + 1).astype(f32)

    twice = 2 * experts
    row_p = iota((twice, 1), 0)
    owner_p = (
        ((z + (row_p // slots) % nz) % nz) * (nx * ny)
        + ((x + row_p // (slots * nz)) % nx) * ny
        + (y + (row_p // 2) % ny) % ny
    )
    owner_two = jnp.concatenate([owner_map[...], owner_map[...]], axis=1)
    half_two = iota((1, twice), 1) // experts
    order_p = ((owner_two == owner_p) & (half_two == row_p % 2)).astype(f32).astype(bf16)

    await_bytes(pk2r, r_pk2)
    both = jnp.maximum(pk2[...], pk2r[...])
    scale_t = (both + 1e-06) / 448.0
    scale = jnp.concatenate([scale_t, jnp.ones((128 - 8, experts), f32)], axis=0).T
    inverse = 1.0 / scale

    def code(c, carry):
        halves = []
        for h in range(2):
            pieces = []
            for j in range(cols):
                field = master[h * parts + c, :, j * 128:(j + 1) * 128]
                pieces.append((snap(field * inverse[:, j:j + 1]) * scale[:, j:j + 1]).astype(bf16))
            halves.append(jnp.concatenate(pieces, axis=1))
        moved = mm(order_p, jnp.concatenate(halves, axis=0))
        moved = moved.astype(bf16).reshape(nx, nz, slots, hid)
        sa[c] = moved
        for dx in range(1, nx):
            send(sa.at[c, dx], c1.at[c, dx], s_cx, r_cx.at[c], x_peer(dx))
        c1[c, 0] = sa[c, 0]
        return carry

    lax.fori_loop(0, parts, code, 0)

    def code_z(c):
        await_bytes(c1.at[c, rest_x], r_cx.at[c])
        for dz in range(1, nz):
            send(c1.at[c, :, dz], c2.at[c, dz], s_cz, r_cz.at[c], group_peer(dz))
        c2[c, 0] = c1[c, :, 0]

    ra_, rb_ = iota((twice, 1), 0), iota((1, twice), 1)
    per_y = 2 * nq
    regroup = (
        rb_ == ((ra_ % per_y) // 2) * slots + (ra_ // per_y) * 2 + ra_ % 2
    ).astype(f32).astype(bf16)

    def code_y(c):
        await_bytes(c2.at[c, rest_z], r_cz.at[c])
        moved = mm(regroup, c2[c].reshape(twice, hid)).astype(bf16).reshape(ny, per_y, hid)
        sb[c] = moved
        for dy in range(1, ny):
            send(sb.at[c, dy], rb.at[c, dy], s_cy, r_cy.at[c], y_peer(dy))
        rb[c, 0] = sb[c, 0]

    row_r = iota((twice, 1), 0)
    source_r = (
        ((z - row_r // (2 * nx) % nz + nz) % nz) * (nx * ny)
        + ((x - (row_r // 2) % nx + nx) % nx) * ny
        + (y - row_r // per_y + ny) % ny
    )
    base_r = source_r * depth + (row_r % 2) * parts
    feature = iota((1, width), 1)

    def place(c):
        await_bytes(rb.at[c, rest_y], r_cy.at[c])
        spread = (feature == base_r + c).astype(f32).astype(bf16)
        piece = lax.dot_general(
            rb[c].reshape(twice, hid), spread, (((0,), (0,)), ((), ())), preferred_element_type=f32
        ).astype(bf16)

        @pl.when(c == 0)
        def _():
            wd[...] = piece

        @pl.when(c > 0)
        def _():
            wd[...] = wd[...] + piece

    def dispatch(s):
        weights = agw[:, s].reshape(line, experts)
        named = (weights > 0).astype(f32)
        ahead = mm(lower, named.astype(bf16))
        turn = (named * (ahead + 1.0)).astype(bf16)
        chosen = (mm_nt(pick, turn) == order_col) & spot
        await_bytes(ag.at[s, rest_y], r_ag.at[s])
        moved = mm(chosen.astype(f32).astype(bf16), ag[s].reshape(line, width))
        xs[s] = moved.astype(bf16).reshape(nx, nz, slots, width)
        for dx in range(1, nx):
            send(xs.at[s, dx], x1.at[s, dx], s_x, r_x.at[s], x_peer(dx))
        x1[s, 0] = xs[s, 0]
        kept = (mm_nt(turn, pick) == order_row) & spot_t
        upper = weights.astype(bf16)
        lesser = (weights - upper.astype(f32)).astype(bf16)
        cmb[s, 0] = jnp.where(kept, mm_nt(upper, pick), 0.0).astype(bf16)
        cmb[s, 1] = jnp.where(kept, mm_nt(lesser, pick), 0.0).astype(bf16)

    def relay(s):
        await_bytes(x1.at[s, rest_x], r_x.at[s])
        for dz in range(1, nz):
            send(x1.at[s, :, dz], xr.at[s, dz], s_z, r_z.at[s], ring_peer(dz, 1))
        xr[s, 0] = x1[s, :, 0]

    def expert_in(s):
        await_bytes(xr.at[s, rest_z], r_z.at[s])
        items = xr[s].reshape(nq * slots, width)
        part[s, 0] = mm(items, gate_up[0])
        part[s, 1] = mm(items, gate_up[1])
        send(part.at[s], partr.at[s], s_grp, r_grp.at[s], grp_mate)

    def expert_mid(s):
        await_bytes(partr.at[s], r_grp.at[s])
        gated = part[s, 0] + partr[s, 0]
        upped = part[s, 1] + partr[s, 1]
        hd[s] = (gated / (1.0 + jnp.exp(-gated)) * upped).astype(bf16)

    def expert_out(s, carry):
        result = mm(hd[s], wd[...])
        ys[s] = result.astype(bf16).reshape(nz, nx, slots, width)
        for dz in range(1, nz):
            send(ys.at[s, dz], z1.at[s, dz], s_rz, r_rz.at[s], ring_peer(dz, -1))
        z1[s, 0] = ys[s, 0]
        return carry

    def relay_back(s):
        await_bytes(z1.at[s, rest_z], r_rz.at[s])
        for dx in range(1, nx):
            send(z1.at[s, :, dx], yr.at[s, dx], s_rx, r_rx.at[s], x_peer(-dx))
        yr[s, 0] = z1[s, :, 0]

    def combine(s):
        await_bytes(yr.at[s, rest_x], r_rx.at[s])
        items = yr[s].reshape(nq * slots, width)
        mixed = mm(cmb[s, 0], items) + mm(cmb[s, 1], items)
        rs[s] = mixed.astype(bf16).reshape(ny, rows, width)
        for dy in range(1, ny):
            send(rs.at[s, dy], rr.at[s, dy], s_rs, r_rs.at[s], y_peer(-dy))
        rr[s, 0] = rs[s, 0]

    def total(s):
        await_bytes(rr.at[s, rest_y], r_rs.at[s])
        mixed = rr[s, 0].astype(f32)
        for dy in range(1, ny):
            mixed += rr[s, dy].astype(f32)
        ts[s] = mixed.astype(bf16)
        send(ts.at[s], tr.at[s], s_tp, r_tp.at[s], tp_mate)

    def finish(s):
        await_bytes(tr.at[s], r_tp.at[s])
        out[s] = (ts[s].astype(f32) + tr[s].astype(f32)).astype(bf16)

    def staged(i, plan, upto):
        for stage, lag in plan:
            @pl.when((i >= lag) & (i < lag + upto))
            def _():
                stage(i - lag)

    await_bytes(agw.at[rest_y], r_agw)

    def forth(i, carry):
        staged(i, [(dispatch, 0), (code_z, 0), (relay, 1), (code_y, 1), (expert_in, 2), (place, 2), (expert_mid, 2)], steps)
        return carry

    def back(i, carry):
        staged(i, [(relay_back, 0), (combine, 1), (total, 2), (finish, 3)], steps)
        return carry

    lax.fori_loop(0, steps + 2, forth, 0)
    lax.fori_loop(0, steps, expert_out, 0)
    lax.fori_loop(0, steps + 3, back, 0)

    await_bytes(agw.at[rest_y], s_agw)
    await_bytes(ag.at[:, rest_y], s_ag)
    await_bytes(pkr.at[rest_y], s_pk)
    await_bytes(pk2r, s_pk2)
    await_bytes(c1.at[:, rest_x], s_cx)
    await_bytes(c2.at[:, rest_z], s_cz)
    await_bytes(rb.at[:, rest_y], s_cy)
    await_bytes(x1.at[:, rest_x], s_x)
    await_bytes(xr.at[:, rest_z], s_z)
    await_bytes(partr, s_grp)
    await_bytes(z1.at[:, rest_z], s_rz)
    await_bytes(yr.at[:, rest_x], s_rx)
    await_bytes(rr.at[:, rest_y], s_rs)
    await_bytes(tr, s_tp)


def on_device(nz, nx, ny, master, gate_up, owner_map, tokens, routes, gate_weights):
    steps, rows, width = tokens.shape
    depth, experts, hid = master.shape
    parts = depth // 2
    nq = nz * nx
    slots = 2 * ny
    line = ny * rows
    vmem = pltpu.VMEM
    dma = pltpu.SemaphoreType.DMA
    by_x = vmem((steps, nx, nz, slots, width), bf16)
    by_z = vmem((steps, nz, nx, slots, width), bf16)
    by_y = vmem((steps, ny, rows, width), bf16)
    sums = vmem((steps, 2, nq * slots, hid), f32)
    own = vmem((steps, rows, width), bf16)
    peak = vmem((8, experts), f32)
    code_x = vmem((parts, nx, nz, slots, hid), bf16)
    code_z = vmem((parts, nz, nx, slots, hid), bf16)
    code_y = vmem((parts, ny, 2 * nq, hid), bf16)
    scratch = [
        vmem((steps, rows, experts), f32),
        vmem((ny, steps, rows, experts), f32),
        by_y, by_x, by_x, by_z,
        vmem((steps, 2, line, nq * slots), bf16),
        sums, sums,
        vmem((steps, nq * slots, hid), bf16),
        by_z, by_z, by_x, by_y, by_y, own, own,
        peak, vmem((ny, 8, experts), f32), peak, peak,
        code_x, code_x, code_z, code_y, code_y,
        vmem((hid, width), bf16),
    ]
    per_step, per_part = dma((steps,)), dma((parts,))
    scratch += [dma] * 14
    scratch += [
        per_step, dma, per_step, per_step, per_step, per_step, per_step, per_step, per_step,
        dma, dma, per_part, per_part, per_part,
    ]
    return pl.pallas_call(
        functools.partial(kernel, nz, nx, ny),
        out_shape=jax.ShapeDtypeStruct((steps, rows, width), bf16),
        in_specs=[pl.BlockSpec(memory_space=vmem)] * 6,
        out_specs=pl.BlockSpec(memory_space=vmem),
        scratch_shapes=scratch,
        compiler_params=pltpu.CompilerParams(
            collective_id=0, has_side_effects=True, vmem_limit_bytes=56 * 2**20
        ),
    )(
        master,
        gate_up[0],
        owner_map.reshape(1, experts),
        tokens,
        jnp.swapaxes(routes, 1, 2),
        jnp.swapaxes(gate_weights, 1, 2),
    )


def solution(mesh, sizes=(4, 4, 8)):
    placed = (
        P(("grp", "ep"), None, "tp"),
        P("ep", None, "grp", "tp"),
        P(),
        P(None, "ep", "grp"),
        P(None, "ep", None),
        P(None, "ep", None),
    )
    return jax.shard_map(
        functools.partial(on_device, *sizes),
        mesh=mesh, in_specs=placed, out_specs=P(None, "ep", "grp"), check_vma=False,
    )
```

time: 154 us -> 128 us (0.83)
  Pallas kernels: 149 us -> 125 us
  local copies, waits for them, and re-layouts: 4.36 us -> 1.57 us
    pallas_call x1, Pallas kernels: 149 us -> 125 us  [on_device(): pl.pallas_call(functools.partial(kernel, nz, nx, ny), out_shape=jax.Shape...]
    unnamed x3 -> x1, local copies, waits for them, and re-layouts: 4.36 us -> 1.57 us
where the time goes in v1:
time: 128 us; the launch traced here: 126 us
  Pallas kernels  125 us (98%)
  local copies, waits for them, and re-layouts  1.57 us (1%)
    pallas_call x1, Pallas kernels, on_device(): pl.pallas_call(functools.partial(kernel, nz, nx, ny), out_shape=jax.Shape...  125 us

profile of v1, /device:TPU:1, one launch (start us, length us, event | category | flops | bytes accessed | tf_op | source)
XLA Modules:
  0.0 126.3 jit_solution(14857709961993016437)
XLA Ops:
  0.0 124.8 %shard_map.64 = bf16[4,16,1024]{2,1,0:T(8,128)(2,1)} custom-call(f32[8,128,384]{2,1,0:T(8,128)} %master.1, bf16[2,1024,384]{2,1,0:T(8,128)(2,1)} %bitcast.4, s32[1,128]{1,0:T(1,128)} %bitcast.7, bf16[4,16,1024]{2,1,0:T(8,128)(2,1)} %tokens.1, s32[4,8,16]{2,1,0:T(8,128)} %bitcast.5, f32[4,8,16]{2,1,0:T(8,128)} %bitcast.6), custom_call_target="tpu_custom_call" | custom-call | tf_op jit(solution)/shard_map/pallas_call | solution.py:386
  124.8 1.6 %copy.8 = bf16[4,16,1024]{2,1,0:T(8,128)(2,1)} copy(bf16[4,16,1024]{2,1,0:T(8,128)(2,1)} %shard_map.64) | data formatting | bytes 262144

commit v2 on v1

--- a/solution.py
+++ b/solution.py
@@ -38,10 +38,10 @@
     nz, nx, ny,
     master, gate_up, owner_map, tokens, routes, gates,
     out,
-    wt, agw, ag, xs, x1, xr, cmb, part, partr, hd, ys, z1, yr, rs, rr, ts, tr,
+    nm, nmr, agw, ag, xs, x1, xr, cmb, part, partr, hd, ys, z1, yr, rs, rr, ts, tr,
     pk, pkr, pk2, pk2r, sa, c1, c2, sb, rb, wd,
-    s_ag, s_agw, s_x, s_z, s_grp, s_rz, s_rx, s_rs, s_tp, s_pk, s_pk2, s_cx, s_cz, s_cy,
-    r_ag, r_agw, r_x, r_z, r_grp, r_rz, r_rx, r_rs, r_tp, r_pk, r_pk2, r_cx, r_cz, r_cy,
+    s_ag, s_nm, s_x, s_z, s_grp, s_rz, s_rx, s_rs, s_tp, s_pk, s_pk2, s_cx, s_cz, s_cy,
+    r_ag, r_nm, r_x, r_z, r_grp, r_rz, r_rx, r_rs, r_tp, r_pk, r_pk2, r_cx, r_cz, r_cy,
 ):
     steps, rows, width = tokens.shape
     experts = owner_map.shape[1]
@@ -111,37 +111,49 @@
         peaks = jnp.where(lanes_p == j, jnp.max(most, axis=1, keepdims=True), peaks)
     pk[...] = peaks.T[:8]
     pkr[0] = pk[...]
+    ag[:, 0] = tokens[...]
 
     count = steps * rows
     blank = [jnp.zeros((top, experts - count), f32)]
-    names = jnp.concatenate([routes[s].astype(f32) for s in range(steps)] + blank, axis=1)
-    shares = jnp.concatenate([gates[s] for s in range(steps)] + blank, axis=1)
-    index_e = iota((experts, experts), 0).astype(f32)
-    weight_of = jnp.zeros((experts, experts), f32)
-    for k in range(top):
-        weight_of += jnp.where(names[k:k + 1, :] == index_e, shares[k:k + 1, :], 0.0)
-    weight_of = weight_of.T[:count].reshape(steps, rows, experts)
-    wt[...] = weight_of
-    agw[0] = weight_of
+    nm[0] = jnp.concatenate([routes[s].astype(f32) for s in range(steps)] + blank, axis=1)
+    nm[1] = jnp.concatenate([gates[s] for s in range(steps)] + blank, axis=1)
+    nmr[0] = nm[...]
     pl.semaphore_wait(barrier, len(greeted))
 
     for dy in range(1, ny):
         send(pk, pkr.at[dy], s_pk, r_pk, y_peer(dy))
-
-    def gather_start(s, carry):
-        for dy in range(1, ny):
-            send(tokens.at[s], ag.at[s, dy], s_ag, r_ag.at[s], y_peer(dy))
-        ag[s, 0] = tokens[s]
-        return carry
-
-    gather_start(0, 0)
     for dy in range(1, ny):
-        send(wt, agw.at[dy], s_agw, r_agw, y_peer(dy))
-
+        send(nm, nmr.at[dy], s_nm, r_nm, y_peer(dy))
+
+    def hop(s, h, sign):
+        held = (h - 1) * sign % ny
+        if h > 1:
+            await_bytes(ag.at[s, held], r_ag.at[s, held])
+        place_at = h * sign % ny
+        send(ag.at[s, held], ag.at[s, place_at], s_ag, r_ag.at[s, place_at], y_peer(sign))
+
+    def ring(h):
+        if 2 * h < ny:
+            def both_ways(s, carry):
+                hop(s, h, 1)
+                hop(s, h, -1)
+                return carry
+
+            lax.fori_loop(0, steps, both_ways, 0)
+        else:
+            for s in range(steps):
+                hop(s, h, 1 - 2 * (s % 2))
+
+    def ring_end(s):
+        await_bytes(ag.at[s, ny // 2], r_ag.at[s, ny // 2])
+        last = ny // 2 + 1 - 2 * (s % 2)
+        await_bytes(ag.at[s, last], r_ag.at[s, last])
+
+    ring(1)
     await_bytes(pkr.at[rest_y], r_pk)
     pk2[...] = jnp.max(pkr[...], axis=0)
     send(pk2, pk2r, s_pk2, r_pk2, x_mate)
-    lax.fori_loop(1, steps, gather_start, 0)
+    ring(2)
 
     row_q = iota((nq * slots, 1), 0)
     peer_q = row_q // slots
@@ -193,13 +205,21 @@
         c1[c, 0] = sa[c, 0]
         return carry
 
-    lax.fori_loop(0, parts, code, 0)
-
     def code_z(c):
         await_bytes(c1.at[c, rest_x], r_cx.at[c])
         for dz in range(1, nz):
             send(c1.at[c, :, dz], c2.at[c, dz], s_cz, r_cz.at[c], group_peer(dz))
         c2[c, 0] = c1[c, :, 0]
+
+    code(0, 0)
+    ring(3)
+    code(1, 0)
+    code_z(0)
+    for h in range(4, ny // 2 + 1):
+        ring(h)
+    code(2, 0)
+    code_z(1)
+    code(3, 0)
 
     ra_, rb_ = iota((twice, 1), 0), iota((1, twice), 1)
     per_y = 2 * nq
@@ -245,7 +265,7 @@
         ahead = mm(lower, named.astype(bf16))
         turn = (named * (ahead + 1.0)).astype(bf16)
         chosen = (mm_nt(pick, turn) == order_col) & spot
-        await_bytes(ag.at[s, rest_y], r_ag.at[s])
+        ring_end(s)
         moved = mm(chosen.astype(f32).astype(bf16), ag[s].reshape(line, width))
         xs[s] = moved.astype(bf16).reshape(nx, nz, slots, width)
         for dx in range(1, nx):
@@ -317,21 +337,34 @@
             def _():
                 stage(i - lag)
 
-    await_bytes(agw.at[rest_y], r_agw)
+    await_bytes(nmr.at[rest_y], r_nm)
+    index_e = iota((experts, experts), 0).astype(f32)
+
+    def spread_weights(dy, carry):
+        names, shares = nmr[dy, 0], nmr[dy, 1]
+        weight_of = jnp.zeros((experts, experts), f32)
+        for k in range(top):
+            weight_of += jnp.where(names[k:k + 1, :] == index_e, shares[k:k + 1, :], 0.0)
+        agw[dy] = weight_of.T[:count].reshape(steps, rows, experts)
+        return carry
+
+    lax.fori_loop(0, ny, spread_weights, 0)
 
     def forth(i, carry):
-        staged(i, [(dispatch, 0), (code_z, 0), (relay, 1), (code_y, 1), (expert_in, 2), (place, 2), (expert_mid, 2)], steps)
+        staged(i, [(dispatch, 0), (code_z, -2), (code_y, 0), (relay, 1), (place, 1), (expert_mid, 3)], steps)
+        first = jnp.where(i < steps + 1, 0, i - steps + 1)
+        lax.fori_loop(first, jnp.where(i < steps, 0, i - steps + 2), expert_out, 0)
+        staged(i, [(expert_in, 2)], steps)
         return carry
 
     def back(i, carry):
         staged(i, [(relay_back, 0), (combine, 1), (total, 2), (finish, 3)], steps)
         return carry
 
-    lax.fori_loop(0, steps + 2, forth, 0)
-    lax.fori_loop(0, steps, expert_out, 0)
+    lax.fori_loop(0, steps + 3, forth, 0)
     lax.fori_loop(0, steps + 3, back, 0)
 
-    await_bytes(agw.at[rest_y], s_agw)
+    await_bytes(nmr.at[rest_y], s_nm)
     await_bytes(ag.at[:, rest_y], s_ag)
     await_bytes(pkr.at[rest_y], s_pk)
     await_bytes(pk2r, s_pk2)
@@ -350,6 +383,7 @@
 def on_device(nz, nx, ny, master, gate_up, owner_map, tokens, routes, gate_weights):
     steps, rows, width = tokens.shape
     depth, experts, hid = master.shape
+    top_rows = routes.shape[2]
     parts = depth // 2
     nq = nz * nx
     slots = 2 * ny
@@ -359,14 +393,15 @@
     by_x = vmem((steps, nx, nz, slots, width), bf16)
     by_z = vmem((steps, nz, nx, slots, width), bf16)
     by_y = vmem((steps, ny, rows, width), bf16)
+    own = vmem((steps, rows, width), bf16)
     sums = vmem((steps, 2, nq * slots, hid), f32)
-    own = vmem((steps, rows, width), bf16)
+    named = vmem((2, top_rows, experts), f32)
     peak = vmem((8, experts), f32)
     code_x = vmem((parts, nx, nz, slots, hid), bf16)
     code_z = vmem((parts, nz, nx, slots, hid), bf16)
     code_y = vmem((parts, ny, 2 * nq, hid), bf16)
     scratch = [
-        vmem((steps, rows, experts), f32),
+        named, vmem((ny, 2, top_rows, experts), f32),
         vmem((ny, steps, rows, experts), f32),
         by_y, by_x, by_x, by_z,
         vmem((steps, 2, line, nq * slots), bf16),
@@ -380,7 +415,7 @@
     per_step, per_part = dma((steps,)), dma((parts,))
     scratch += [dma] * 14
     scratch += [
-        per_step, dma, per_step, per_step, per_step, per_step, per_step, per_step, per_step,
+        dma((steps, ny)), dma, per_step, per_step, per_step, per_step, per_step, per_step, per_step,
         dma, dma, per_part, per_part, per_part,
     ]
     return pl.pallas_call(

time: 128 us -> 119 us (0.930)
  the two profiles are of different devices: /device:TPU:1 before, /device:TPU:26 now
where the time goes in v2:
time: 119 us
  Pallas kernels  118 us (99%)
  local copies, waits for them, and re-layouts  1.57 us (1%)
    pallas_call x1, Pallas kernels, on_device(): pl.pallas_call(functools.partial(kernel, nz, nx, ny), out_shape=jax.Shape...  118 us

profile of v2, /device:TPU:26, one launch (start us, length us, event | category | flops | bytes accessed | tf_op | source)
XLA Modules:
  0.0 119.1 jit_solution(18049991437480155548)
XLA Ops:
  0.0 117.6 %shard_map.64 = bf16[4,16,1024]{2,1,0:T(8,128)(2,1)} custom-call(f32[8,128,384]{2,1,0:T(8,128)} %master.1, bf16[2,1024,384]{2,1,0:T(8,128)(2,1)} %bitcast.4, s32[1,128]{1,0:T(1,128)} %bitcast.7, bf16[4,16,1024]{2,1,0:T(8,128)(2,1)} %tokens.1, s32[4,8,16]{2,1,0:T(8,128)} %bitcast.5, f32[4,8,16]{2,1,0:T(8,128)} %bitcast.6), custom_call_target="tpu_custom_call" | custom-call | tf_op jit(solution)/shard_map/pallas_call | solution.py:421
  117.6 1.6 %copy.8 = bf16[4,16,1024]{2,1,0:T(8,128)(2,1)} copy(bf16[4,16,1024]{2,1,0:T(8,128)(2,1)} %shard_map.64) | data formatting | bytes 262144

commit v3 on v2

--- a/solution.py
+++ b/solution.py
@@ -38,7 +38,7 @@
     nz, nx, ny,
     master, gate_up, owner_map, tokens, routes, gates,
     out,
-    nm, nmr, agw, ag, xs, x1, xr, cmb, part, partr, hd, ys, z1, yr, rs, rr, ts, tr,
+    nm, nmr, agw, ag, xs, x1, xr, cmb, part, partr, hd, ys, x2, yr, rs, rr, ts, tr,
     pk, pkr, pk2, pk2r, sa, c1, c2, sb, rb, wd,
     s_ag, s_nm, s_x, s_z, s_grp, s_rz, s_rx, s_rs, s_tp, s_pk, s_pk2, s_cx, s_cz, s_cy,
     r_ag, r_nm, r_x, r_z, r_grp, r_rz, r_rx, r_rs, r_tp, r_pk, r_pk2, r_cx, r_cz, r_cy,
@@ -51,6 +51,7 @@
     nq = nz * nx
     slots = 2 * ny
     line = ny * rows
+    wide = width // 2
     g = lax.axis_index("grp")
     ep = lax.axis_index("ep")
     t = lax.axis_index("tp")
@@ -161,6 +162,10 @@
         ((z + peer_q % nz) % nz) * (nx * ny) + ((x + peer_q // nz) % nx) * ny + y
     )
     pick = (owner_map[...] == owner_q).astype(f32).astype(bf16)
+    owner_b = (
+        ((z + peer_q // nx) % nz) * (nx * ny) + ((x + peer_q % nx) % nx) * ny + y
+    )
+    pick_back = (owner_map[...] == owner_b).astype(f32).astype(bf16)
     slot_col = row_q % slots
     slot_row = iota((1, nq * slots), 1) % slots
     row_col = iota((line, 1), 0) // rows
@@ -253,11 +258,13 @@
 
         @pl.when(c == 0)
         def _():
-            wd[...] = piece
+            for v in range(2):
+                wd[v] = piece[:, v * wide:(v + 1) * wide]
 
         @pl.when(c > 0)
         def _():
-            wd[...] = wd[...] + piece
+            for v in range(2):
+                wd[v] = wd[v] + piece[:, v * wide:(v + 1) * wide]
 
     def dispatch(s):
         weights = agw[:, s].reshape(line, experts)
@@ -271,11 +278,11 @@
         for dx in range(1, nx):
             send(xs.at[s, dx], x1.at[s, dx], s_x, r_x.at[s], x_peer(dx))
         x1[s, 0] = xs[s, 0]
-        kept = (mm_nt(turn, pick) == order_row) & spot_t
+        kept = (mm_nt(turn, pick_back) == order_row) & spot_t
         upper = weights.astype(bf16)
         lesser = (weights - upper.astype(f32)).astype(bf16)
-        cmb[s, 0] = jnp.where(kept, mm_nt(upper, pick), 0.0).astype(bf16)
-        cmb[s, 1] = jnp.where(kept, mm_nt(lesser, pick), 0.0).astype(bf16)
+        cmb[s, 0] = jnp.where(kept, mm_nt(upper, pick_back), 0.0).astype(bf16)
+        cmb[s, 1] = jnp.where(kept, mm_nt(lesser, pick_back), 0.0).astype(bf16)
 
     def relay(s):
         await_bytes(x1.at[s, rest_x], r_x.at[s])
@@ -297,39 +304,42 @@
         hd[s] = (gated / (1.0 + jnp.exp(-gated)) * upped).astype(bf16)
 
     def expert_out(s, carry):
-        result = mm(hd[s], wd[...])
-        ys[s] = result.astype(bf16).reshape(nz, nx, slots, width)
+        for v in range(2):
+            u = 2 * s + v
+            ys[u] = mm(hd[s], wd[v]).astype(bf16).reshape(nz, nx, slots, wide)
+            for dx in range(1, nx):
+                send(ys.at[u, :, dx], x2.at[u, dx], s_rx, r_rx.at[u], x_peer(-dx))
+            x2[u, 0] = ys[u, :, 0]
+        return carry
+
+    def relay_back(u):
+        await_bytes(x2.at[u, rest_x], r_rx.at[u])
         for dz in range(1, nz):
-            send(ys.at[s, dz], z1.at[s, dz], s_rz, r_rz.at[s], ring_peer(dz, -1))
-        z1[s, 0] = ys[s, 0]
-        return carry
-
-    def relay_back(s):
-        await_bytes(z1.at[s, rest_z], r_rz.at[s])
-        for dx in range(1, nx):
-            send(z1.at[s, :, dx], yr.at[s, dx], s_rx, r_rx.at[s], x_peer(-dx))
-        yr[s, 0] = z1[s, :, 0]
-
-    def combine(s):
-        await_bytes(yr.at[s, rest_x], r_rx.at[s])
-        items = yr[s].reshape(nq * slots, width)
+            send(x2.at[u, :, dz], yr.at[u, dz], s_rz, r_rz.at[u], ring_peer(dz, -1))
+        yr[u, 0] = x2[u, :, 0]
+
+    def combine(u):
+        await_bytes(yr.at[u, rest_z], r_rz.at[u])
+        items = yr[u].reshape(nq * slots, wide)
+        s = u // 2
         mixed = mm(cmb[s, 0], items) + mm(cmb[s, 1], items)
-        rs[s] = mixed.astype(bf16).reshape(ny, rows, width)
+        rs[u] = mixed.astype(bf16).reshape(ny, rows, wide)
         for dy in range(1, ny):
-            send(rs.at[s, dy], rr.at[s, dy], s_rs, r_rs.at[s], y_peer(-dy))
-        rr[s, 0] = rs[s, 0]
-
-    def total(s):
-        await_bytes(rr.at[s, rest_y], r_rs.at[s])
-        mixed = rr[s, 0].astype(f32)
+            send(rs.at[u, dy], rr.at[u, dy], s_rs, r_rs.at[u], y_peer(-dy))
+        rr[u, 0] = rs[u, 0]
+
+    def total(u):
+        await_bytes(rr.at[u, rest_y], r_rs.at[u])
+        mixed = rr[u, 0].astype(f32)
         for dy in range(1, ny):
-            mixed += rr[s, dy].astype(f32)
-        ts[s] = mixed.astype(bf16)
-        send(ts.at[s], tr.at[s], s_tp, r_tp.at[s], tp_mate)
-
-    def finish(s):
-        await_bytes(tr.at[s], r_tp.at[s])
-        out[s] = (ts[s].astype(f32) + tr[s].astype(f32)).astype(bf16)
+            mixed += rr[u, dy].astype(f32)
+        ts[u] = mixed.astype(bf16)
+        send(ts.at[u], tr.at[u], s_tp, r_tp.at[u], tp_mate)
+
+    def finish(u):
+        await_bytes(tr.at[u], r_tp.at[u])
+        at = pl.ds(pl.multiple_of((u % 2) * wide, wide), wide)
+        out[u // 2, :, at] = (ts[u].astype(f32) + tr[u].astype(f32)).astype(bf16)
 
     def staged(i, plan, upto):
         for stage, lag in plan:
@@ -351,18 +361,18 @@
     lax.fori_loop(0, ny, spread_weights, 0)
 
     def forth(i, carry):
-        staged(i, [(dispatch, 0), (code_z, -2), (code_y, 0), (relay, 1), (place, 1), (expert_mid, 3)], steps)
-        first = jnp.where(i < steps + 1, 0, i - steps + 1)
-        lax.fori_loop(first, jnp.where(i < steps, 0, i - steps + 2), expert_out, 0)
-        staged(i, [(expert_in, 2)], steps)
+        staged(i, [(dispatch, 0), (code_z, -2), (code_y, 0), (relay, 1), (place, 2), (expert_mid, 4)], steps)
+        first = jnp.where(i < 6, 0, i - 4)
+        lax.fori_loop(first, jnp.where(i < 5, 0, i - 3), expert_out, 0)
+        staged(i, [(expert_in, 3)], steps)
         return carry
 
     def back(i, carry):
-        staged(i, [(relay_back, 0), (combine, 1), (total, 2), (finish, 3)], steps)
+        staged(i, [(relay_back, 0), (combine, 2), (total, 4), (finish, 6)], 2 * steps)
         return carry
 
-    lax.fori_loop(0, steps + 3, forth, 0)
-    lax.fori_loop(0, steps + 3, back, 0)
+    lax.fori_loop(0, steps + 4, forth, 0)
+    lax.fori_loop(0, 2 * steps + 6, back, 0)
 
     await_bytes(nmr.at[rest_y], s_nm)
     await_bytes(ag.at[:, rest_y], s_ag)
@@ -374,8 +384,8 @@
     await_bytes(x1.at[:, rest_x], s_x)
     await_bytes(xr.at[:, rest_z], s_z)
     await_bytes(partr, s_grp)
-    await_bytes(z1.at[:, rest_z], s_rz)
-    await_bytes(yr.at[:, rest_x], s_rx)
+    await_bytes(x2.at[:, rest_x], s_rx)
+    await_bytes(yr.at[:, rest_z], s_rz)
     await_bytes(rr.at[:, rest_y], s_rs)
     await_bytes(tr, s_tp)
 
@@ -390,10 +400,13 @@
     line = ny * rows
     vmem = pltpu.VMEM
     dma = pltpu.SemaphoreType.DMA
+    wide = width // 2
     by_x = vmem((steps, nx, nz, slots, width), bf16)
     by_z = vmem((steps, nz, nx, slots, width), bf16)
-    by_y = vmem((steps, ny, rows, width), bf16)
-    own = vmem((steps, rows, width), bf16)
+    back_x = vmem((2 * steps, nx, nz, slots, wide), bf16)
+    back_z = vmem((2 * steps, nz, nx, slots, wide), bf16)
+    back_y = vmem((2 * steps, ny, rows, wide), bf16)
+    back_own = vmem((2 * steps, rows, wide), bf16)
     sums = vmem((steps, 2, nq * slots, hid), f32)
     named = vmem((2, top_rows, experts), f32)
     peak = vmem((8, experts), f32)
@@ -403,19 +416,20 @@
     scratch = [
         named, vmem((ny, 2, top_rows, experts), f32),
         vmem((ny, steps, rows, experts), f32),
-        by_y, by_x, by_x, by_z,
+        vmem((steps, ny, rows, width), bf16),
+        by_x, by_x, by_z,
         vmem((steps, 2, line, nq * slots), bf16),
         sums, sums,
         vmem((steps, nq * slots, hid), bf16),
-        by_z, by_z, by_x, by_y, by_y, own, own,
+        back_z, back_x, back_z, back_y, back_y, back_own, back_own,
         peak, vmem((ny, 8, experts), f32), peak, peak,
         code_x, code_x, code_z, code_y, code_y,
-        vmem((hid, width), bf16),
+        vmem((2, hid, wide), bf16),
     ]
-    per_step, per_part = dma((steps,)), dma((parts,))
+    per_step, per_part, per_half = dma((steps,)), dma((parts,)), dma((2 * steps,))
     scratch += [dma] * 14
     scratch += [
-        dma((steps, ny)), dma, per_step, per_step, per_step, per_step, per_step, per_step, per_step,
+        dma((steps, ny)), dma, per_step, per_step, per_step, per_half, per_half, per_half, per_half,
         dma, dma, per_part, per_part, per_part,
     ]
     return pl.pallas_call(

time: 119 us -> 114 us (0.958)
  the two profiles are of different devices: /device:TPU:26 before, /device:TPU:1 now
where the time goes in v3:
time: 114 us; the launch traced here: 113 us
  Pallas kernels  112 us (98%)
  local copies, waits for them, and re-layouts  1.57 us (1%)
    pallas_call x1, Pallas kernels, on_device(): pl.pallas_call(functools.partial(kernel, nz, nx, ny), out_shape=jax.Shape...  112 us

profile of v3, /device:TPU:1, one launch (start us, length us, event | category | flops | bytes accessed | tf_op | source)
XLA Modules:
  0.0 113.3 jit_solution(15586244111809862910)
XLA Ops:
  0.0 111.7 %shard_map.64 = bf16[4,16,1024]{2,1,0:T(8,128)(2,1)} custom-call(f32[8,128,384]{2,1,0:T(8,128)} %master.1, bf16[2,1024,384]{2,1,0:T(8,128)(2,1)} %bitcast.4, s32[1,128]{1,0:T(1,128)} %bitcast.7, bf16[4,16,1024]{2,1,0:T(8,128)(2,1)} %tokens.1, s32[4,8,16]{2,1,0:T(8,128)} %bitcast.5, f32[4,8,16]{2,1,0:T(8,128)} %bitcast.6), custom_call_target="tpu_custom_call" | custom-call | tf_op jit(solution)/shard_map/pallas_call | solution.py:435
  111.7 1.6 %copy.8 = bf16[4,16,1024]{2,1,0:T(8,128)(2,1)} copy(bf16[4,16,1024]{2,1,0:T(8,128)(2,1)} %shard_map.64) | data formatting | bytes 262144

commit v4 on v3

--- a/solution.py
+++ b/solution.py
@@ -36,12 +36,12 @@
 
 def kernel(
     nz, nx, ny,
-    master, gate_up, owner_map, tokens, routes, gates,
-    out,
+    master_in, gate_up_in, owner_map, tokens, routes, gates,
+    out, master, gate_up,
     nm, nmr, agw, ag, xs, x1, xr, cmb, part, partr, hd, ys, x2, yr, rs, rr, ts, tr,
     pk, pkr, pk2, pk2r, sa, c1, c2, sb, rb, wd,
     s_ag, s_nm, s_x, s_z, s_grp, s_rz, s_rx, s_rs, s_tp, s_pk, s_pk2, s_cx, s_cz, s_cy,
-    r_ag, r_nm, r_x, r_z, r_grp, r_rz, r_rx, r_rs, r_tp, r_pk, r_pk2, r_cx, r_cz, r_cy,
+    in_m, in_g, r_ag, r_nm, r_x, r_z, r_grp, r_rz, r_rx, r_rs, r_tp, r_pk, r_pk2, r_cx, r_cz, r_cy,
 ):
     steps, rows, width = tokens.shape
     experts = owner_map.shape[1]
@@ -91,6 +91,11 @@
     for peer in greeted:
         pl.semaphore_signal(barrier, inc=1, device_id=peer, device_id_type=pl.DeviceIdType.MESH)
 
+    load_m = pltpu.make_async_copy(master_in, master, in_m)
+    load_g = pltpu.make_async_copy(gate_up_in, gate_up, in_g)
+    load_m.start()
+    load_g.start()
+
     def send(src, dst, ssem, rsem, peer):
         pltpu.make_async_remote_copy(
             src_ref=src, dst_ref=dst, send_sem=ssem, recv_sem=rsem,
@@ -102,6 +107,7 @@
 
     rest_x, rest_y, rest_z = pl.ds(1, nx - 1), pl.ds(1, ny - 1), pl.ds(1, nz - 1)
 
+    load_m.wait()
     cols = hid // 128
     lanes_p = iota((experts, 128), 1)
     peaks = jnp.zeros((experts, 128), f32)
@@ -368,11 +374,12 @@
         return carry
 
     def back(i, carry):
-        staged(i, [(relay_back, 0), (combine, 2), (total, 4), (finish, 6)], 2 * steps)
+        staged(i, [(relay_back, 0), (combine, 3), (total, 6), (finish, 8)], 2 * steps)
         return carry
 
+    load_g.wait()
     lax.fori_loop(0, steps + 4, forth, 0)
-    lax.fori_loop(0, 2 * steps + 6, back, 0)
+    lax.fori_loop(0, 2 * steps + 8, back, 0)
 
     await_bytes(nmr.at[rest_y], s_nm)
     await_bytes(ag.at[:, rest_y], s_ag)
@@ -414,6 +421,7 @@
     code_z = vmem((parts, nz, nx, slots, hid), bf16)
     code_y = vmem((parts, ny, 2 * nq, hid), bf16)
     scratch = [
+        vmem(master.shape, f32), vmem(gate_up.shape[1:], bf16),
         named, vmem((ny, 2, top_rows, experts), f32),
         vmem((ny, steps, rows, experts), f32),
         vmem((steps, ny, rows, width), bf16),
@@ -427,7 +435,7 @@
         vmem((2, hid, wide), bf16),
     ]
     per_step, per_part, per_half = dma((steps,)), dma((parts,)), dma((2 * steps,))
-    scratch += [dma] * 14
+    scratch += [dma] * 16
     scratch += [
         dma((steps, ny)), dma, per_step, per_step, per_step, per_half, per_half, per_half, per_half,
         dma, dma, per_part, per_part, per_part,
@@ -435,7 +443,7 @@
     return pl.pallas_call(
         functools.partial(kernel, nz, nx, ny),
         out_shape=jax.ShapeDtypeStruct((steps, rows, width), bf16),
-        in_specs=[pl.BlockSpec(memory_space=vmem)] * 6,
+        in_specs=[pl.BlockSpec(memory_space=pl.ANY)] * 2 + [pl.BlockSpec(memory_space=vmem)] * 4,
         out_specs=pl.BlockSpec(memory_space=vmem),
         scratch_shapes=scratch,
         compiler_params=pltpu.CompilerParams(

time: 114 us -> 112 us (0.982)
  no operation moved by 1% of the time
where the time goes in v4:
time: 112 us
  Pallas kernels  111 us (99%)
  local copies, waits for them, and re-layouts  1.57 us (1%)
    pallas_call x1, Pallas kernels, on_device(): pl.pallas_call(functools.partial(kernel, nz, nx, ny), out_shape=jax.Shape...  111 us

profile of v4, /device:TPU:1, one launch (start us, length us, event | category | flops | bytes accessed | tf_op | source)
XLA Modules:
  0.0 112.3 jit_solution(12932920995647846022)
XLA Ops:
  0.0 110.8 %shard_map.64 = bf16[4,16,1024]{2,1,0:T(8,128)(2,1)} custom-call(f32[8,128,384]{2,1,0:T(8,128)} %master_in.1, bf16[2,1024,384]{2,1,0:T(8,128)(2,1)} %bitcast.4, s32[1,128]{1,0:T(1,128)} %bitcast.7, bf16[4,16,1024]{2,1,0:T(8,128)(2,1)} %tokens.1, s32[4,8,16]{2,1,0:T(8,128)} %bitcast.5, f32[4,8,16]{2,1,0:T(8,128)} %bitcast.6), custom_call_target="tpu_custom_call" | custom-call | tf_op jit(solution)/shard_map/pallas_call | solution.py:443
  110.8 1.6 %copy.8 = bf16[4,16,1024]{2,1,0:T(8,128)(2,1)} copy(bf16[4,16,1024]{2,1,0:T(8,128)(2,1)} %shard_map.64) | data formatting | bytes 262144
